TPU v7x, 256 devices: a whole 4x4x8 slice. The times are simulated.
256 devices in a mesh: row: 16 (over z, y_lo), col: 16 (over x, y_hi, core).
Axes of the slice: x: 4, y: 4 (y_hi: 2, y_lo: 2; y = y_hi * 2 + y_lo), z: 8, core: 2. Of those that a mesh axis runs over, the one named last changes fastest.
Arguments:
- memory: bfloat16 [8192, 4096], P('row', 'col'), may hold values from -0.09375 to 0.09375
- joined_weight: bfloat16 [2, 4096, 8192], P(None, 'row', 'col'), may hold values from -0.09375 to 0.09375
- joined_cotangent: bfloat16 [2, 8192, 8192], P(None, 'row', 'col'), may hold values from -6 to 6
Outputs:
- memory_grad: bfloat16 [8192, 4096], P('row', 'col')
- weight_grad: float32 [2, 4096, 8192], P(None, 'row', 'col')
All inputs are finite; a program needn't handle non-finite values.
Results may differ from a plain program's by a relative error of at most 0.001.
Values may be sent and summed in bfloat16 or wider, within the bound.
A program may use at most 128 MiB of HBM per device.

v0:
```python
from functools import partial

import jax
import jax.numpy as jnp
from jax import lax
from jax.sharding import PartitionSpec as P


def layer_term(memory_row, cotangent, first_row, row_count):
    return lax.dot_general(
        memory_row, cotangent, (((0,), (0,)), ((), ())), preferred_element_type=jnp.float32
    )


def on_device(memory, joined_weight, joined_cotangent):
    partial_memory = jnp.einsum(
        "lrf,lnf->rn",
        joined_cotangent,
        lax.all_gather(joined_weight, "row", axis=1, tiled=True),
        preferred_element_type=jnp.float32,
    )
    memory_grad = lax.psum_scatter(partial_memory, "col", scatter_dimension=1, tiled=True).astype(
        jnp.bfloat16
    )
    memory_row = lax.all_gather(memory, "col", axis=1, tiled=True)
    results = []
    for layer_index in range(joined_cotangent.shape[0]):
        term_fn = partial(layer_term, memory_row, joined_cotangent[layer_index])
        results.append(
            lax.psum_scatter(
                term_fn(jnp.int32(0), joined_weight.shape[1] * lax.axis_size("row")),
                "row",
                scatter_dimension=0,
                tiled=True,
            )
        )
    weight_grad = jnp.stack(results)
    return (memory_grad, weight_grad)


def solution(mesh):
    in_specs = (P("row", "col"), P(None, "row", "col"), P(None, "row", "col"))
    out_specs = (P("row", "col"), P(None, "row", "col"))
    return jax.shard_map(
        on_device, mesh=mesh, in_specs=in_specs, out_specs=out_specs, check_vma=False
    )
```

profile of v0, /device:TPU:4, one launch (start us, length us, event | category | flops | bytes accessed | tf_op | source)
XLA Modules:
  0.0 755.3 jit_solution(15783643282875729734)
XLA Ops:
  7.2 0.0 all-gather.5.cloned.1.call-start
  7.2 0.7 all-gather.5.cloned.1.call-update
  7.9 0.0 all-gather.3.cloned.1.call-start
  7.9 0.7 all-gather.3.cloned.1.call-update
  8.6 0.0 copy-start
  8.7 0.0 reduce-scatter.8.cloned.1.call-start
  8.7 67.4 %all-gather.5.cloned.1.call-done = bf16[512,4096]{1,0:T(8,128)(2,1)} async-done(((bf16[512,256]{1,0:T(8,128)(2,1)}), bf16[512,4096]{1,0:T(8,128)(2,1)}) %all-gather.5.cloned.1.call-update) | async-done | bytes 4194320 | tf_op jit(solution)/shard_map/all_gather | solution.py:25
  76.1 7.9 %fusion = f32[4096,512]{1,0:T(8,128)} fusion(bf16[512,4096]{1,0:T(8,128)(2,1)} %all-gather.5.cloned.1.call-done, bf16[2,512,512]{2,1,0:T(8,128)(2,1)} %param.5), kind=kOutput, calls=%fused_computation.2 | convolution fusion | flops 2147483648 | bytes 13107200 | tf_op jit(solution)/shard_map/dot_general | solution.py:10
  84.0 0.0 reduce-scatter.8.cloned.1.call-update
  84.0 0.0 reduce-scatter.6.cloned.1.call-start
  84.1 0.0 copy-done
  84.1 7.8 %fusion.2 = f32[4096,512]{1,0:T(8,128)} fusion(bf16[512,4096]{1,0:T(8,128)(2,1)} %all-gather.5.cloned.1.call-done, bf16[2,512,512]{2,1,0:T(8,128)(2,1)S(1)} %copy-done), kind=kOutput, calls=%fused_computation.4 | convolution fusion | flops 2147483648 | bytes 13107200 | tf_op jit(solution)/shard_map/dot_general | solution.py:10
  91.9 0.0 reduce-scatter.6.cloned.1.call-update
  91.9 0.0 reduce-scatter.4.cloned.1.call-start
  91.9 168.8 %all-gather.3.cloned.1.call-done = bf16[2,4096,512]{2,1,0:T(8,128)(2,1)} async-done(((bf16[2,256,512]{2,1,0:T(8,128)(2,1)}), bf16[2,4096,512]{2,1,0:T(8,128)(2,1)}) %all-gather.3.cloned.1.call-update) | async-done | bytes 8388624 | tf_op jit(solution)/shard_map/all_gather | solution.py:19
  260.7 10.1 %convolution_bitcast_fusion = f32[512,4096]{1,0:T(8,128)} fusion(bf16[2,512,512]{2,1,0:T(8,128)(2,1)S(1)} %copy-done, bf16[2,4096,512]{2,1,0:T(8,128)(2,1)} %all-gather.3.cloned.1.call-done), kind=kOutput, calls=%fused_computation | convolution fusion | flops 4294967296 | bytes 17825792 | tf_op jit(solution)/shard_map/lrf,lnf->rn/dot_general | solution.py:16
  270.8 0.0 reduce-scatter.4.cloned.1.call-update
  270.9 176.0 %reduce-scatter.8.cloned.1.call-done = f32[256,512]{1,0:T(8,128)} async-done(((f32[4096,512]{1,0:T(8,128)}), f32[256,512]{1,0:T(8,128)}) %reduce-scatter.8.cloned.1.call-update) | async-done | bytes 524304 | tf_op jit(solution)/shard_map/reduce_scatter | solution.py:30
  446.8 186.0 %reduce-scatter.6.cloned.1.call-done = f32[256,512]{1,0:T(8,128)} async-done(((f32[4096,512]{1,0:T(8,128)}), f32[256,512]{1,0:T(8,128)}) %reduce-scatter.6.cloned.1.call-update) | async-done | bytes 524304 | tf_op jit(solution)/shard_map/reduce_scatter | solution.py:30
  632.8 2.2 pad_maximum_fusion
  635.1 111.9 %reduce-scatter.4.cloned.1.call-done = f32[512,256]{1,0:T(8,128)} async-done(((f32[512,4096]{1,0:T(8,128)}), f32[512,256]{1,0:T(8,128)}) %reduce-scatter.4.cloned.1.call-update) | async-done | bytes 524304 | tf_op jit(solution)/shard_map/reduce_scatter | solution.py:22
  747.0 1.8 convert_element_type.3
Async XLA Ops:
  7.2 68.9 %all-gather.5.cloned.1.call-start = ((), (), s32[]{:S(2)}) async-start(), calls=%async_computation.5 | async-start | bytes 4456448 | tf_op jit(solution)/shard_map/all_gather | solution.py:25
  7.9 252.8 %all-gather.3.cloned.1.call-start = ((), (), s32[]{:S(2)}) async-start(), calls=%async_computation.3 | async-start | bytes 8912896 | tf_op jit(solution)/shard_map/all_gather | solution.py:19
  8.6 75.4 %copy-start = (bf16[2,512,512]{2,1,0:T(8,128)(2,1)S(1)}, bf16[2,512,512]{2,1,0:T(8,128)(2,1)}, u32[]{:S(2)}) copy-start(bf16[2,512,512]{2,1,0:T(8,128)(2,1)} %param.5) | copy-start | bytes 3145732
  8.7 438.2 %reduce-scatter.8.cloned.1.call-start = ((), (), s32[]{:S(2)}) async-start(), calls=%async_computation.7 | async-start | bytes 8912896 | tf_op jit(solution)/shard_map/reduce_scatter | solution.py:30
  84.0 548.8 %reduce-scatter.6.cloned.1.call-start = ((), (), s32[]{:S(2)}) async-start(), calls=%async_computation.6 | async-start | bytes 8912896 | tf_op jit(solution)/shard_map/reduce_scatter | solution.py:30
  91.9 655.1 %reduce-scatter.4.cloned.1.call-start = ((), (), s32[]{:S(2)}) async-start(), calls=%async_computation.4 | async-start | bytes 8912896 | tf_op jit(solution)/shard_map/reduce_scatter | solution.py:22
Sparse Core Ops, SparseCore 0:
  10.5 65.4 all-gather.4
  77.8 182.8 all-gather.2
  263.3 183.5 reduce-scatter.7
  449.2 183.5 reduce-scatter.5
  637.3 109.6 reduce-scatter.3
where the time goes:
time: 757 us; the launch traced here: 755 us
  waiting for transfers between devices  711 us (94%)
  matrix products  25.8 us (3%)
  between operations  13.8 us (2%)
    reduce_scatter x2, waiting for transfers between devices, on_device(): lax.psum_scatter(term_fn(jnp.int32(0), joined_weight.shape[1] * lax.axis_...  362 us
    all_gather x1, waiting for transfers between devices, on_device(): lax.all_gather(joined_weight, 'row', axis=1, tiled=True)  169 us
    reduce_scatter x1, waiting for transfers between devices, on_device(): lax.psum_scatter(partial_memory, 'col', scatter_dimension=1, tiled=True)  112 us
    all_gather x1, waiting for transfers between devices, on_device(): memory_row = lax.all_gather(memory, 'col', axis=1, tiled=True)  67.4 us
    dot_general x2, matrix products, layer_term(): lax.dot_general(memory_row, cotangent, (((0,), (0,)), ((), ())), preferre...  15.7 us
  transfers between devices with their start and end apart: 5, of which 5 were waited for; matrix products, arithmetic and copies ran while one was open for 4% of the time, Pallas kernels for 0%

commit v1 on v0

v1 whole, which is shorter than its diff:
```python
import jax
import jax.numpy as jnp
from jax import lax
from jax.experimental import pallas as pl
from jax.experimental.pallas import tpu as pltpu
from jax.sharding import PartitionSpec as P

MESH = pl.DeviceIdType.MESH
F32 = jnp.float32
ORDER = (0, 7, 1, 6, 2, 5, 3, 4)


def dot_nt(a, b):
    return lax.dot_general(a, b, (((1,), (1,)), ((), ())), preferred_element_type=F32)


def dot_tn(a, b):
    return lax.dot_general(a, b, (((0,), (0,)), ((), ())), preferred_element_type=F32)


def kernel(
    m_ref, w_ref, c_ref, mg_ref, wg_ref,
    c_all, w_all, m_all, p_own, p_send, p_recv, x_recv, s_own, y_recv, o_send, acc, wg_recv,
    c_ss, c_rs, w_ss, w_rs, m1_ss, m1_rs, m2_ss, m2_rs, m3_ss, p_ss, p_rs, x_ss, x_rs, y_ss, y_rs,
    o_ss, o_rs, g_ss, g_rs,
):
    row, col = lax.axis_index("row"), lax.axis_index("col")
    z, b = lax.div(row, 2), lax.rem(row, 2)
    k, core = lax.div(col, 2), lax.rem(col, 2)
    x, h = lax.div(k, 2), lax.rem(k, 2)
    up = (lax.rem(z + 1, 8) * 2 + b, col)
    down = (lax.rem(z + 7, 8) * 2 + b, col)
    y_pair = (z * 2 + 1 - b, col)
    core_pair = (row, k * 2 + 1 - core)
    h_pair = (row, (x * 2 + 1 - h) * 2 + core)
    xs = [lax.rem(x + o, 4) for o in range(4)]
    x_peer = [(row, (xs[o] * 2 + h) * 2 + core) for o in range(4)]
    ks = [lax.rem(k + o, 8) for o in range(8)]
    zs = [lax.rem(z + o, 8) for o in range(8)]
    plane_peer = [(k * 2 + b, ks[o] * 2 + core) for o in range(8)]
    line_peer = [(zs[o] * 2 + b, z * 2 + core) for o in range(8)]
    diagonal = z == k

    barrier = pltpu.get_barrier_semaphore()
    greeted = [up, down, y_pair, core_pair, h_pair] + x_peer[1:] + plane_peer + line_peer
    for peer in greeted:
        pl.semaphore_signal(barrier, inc=1, device_id=peer, device_id_type=MESH)
    pl.semaphore_wait(barrier, len(greeted))

    sent = []

    def send(src, dst, ss, rs, peer):
        copy = pltpu.make_async_remote_copy(
            src_ref=src, dst_ref=dst, send_sem=ss, recv_sem=rs, device_id=peer, device_id_type=MESH
        )
        copy.start()
        sent.append(copy)

    def arrived(dst, rs):
        pltpu.make_async_copy(dst, dst, rs).wait()

    slot = lax.rem(z - k + 8, 8)
    m1 = []
    for o in range(8):
        src = m_ref.at[pl.ds(pl.multiple_of(ks[o] * 64, 64), 64), :]
        dst = m_all.at[core, ks[o], slot]
        copy = pltpu.make_async_remote_copy(
            src_ref=src, dst_ref=dst, send_sem=m1_ss.at[o], recv_sem=m1_rs.at[slot],
            device_id=plane_peer[o], device_id_type=MESH,
        )
        if o == 0:
            own = pltpu.make_async_copy(src, dst, m1_rs.at[slot])
            pl.when(diagonal)(own.start)
            pl.when(jnp.logical_not(diagonal))(copy.start)
        else:
            copy.start()
        m1.append(copy)

    send(w_ref, w_all.at[b], w_ss, w_rs, y_pair)

    def c_src(offset, l):
        return c_ref.at[l] if offset == 0 else c_all.at[offset, l]

    def c_step(step, l):
        if step < 4 or l == 0:
            src = (8 - (step - 1)) % 8
            send(c_src(src, l), c_all.at[8 - step, l], c_ss.at[0, step - 1, l], c_rs.at[0, step - 1, l], up)
        if step < 4 or l == 1:
            send(c_src(step - 1, l), c_all.at[step, l], c_ss.at[1, step - 1, l], c_rs.at[1, step - 1, l], down)

    def c_wait(step, l):
        if step < 4 or l == 0:
            arrived(c_all.at[8 - step, l], c_rs.at[0, step - 1, l])
        if step < 4 or l == 1:
            arrived(c_all.at[step, l], c_rs.at[1, step - 1, l])

    c_step(1, 0)
    c_step(1, 1)
    w_all[b] = w_ref[...]

    for o in range(8):
        arrived(m_all.at[core, k, o], m1_rs.at[o])
    kh = x * 2 + 1 - h

    def share(piece, ss, to_h):
        ref = m_all.at[core, piece]
        if to_h:
            send(ref, ref, m2_ss.at[ss], m2_rs.at[core, piece], h_pair)
        for o in (1, 3, 2):
            send(ref, ref, m2_ss.at[ss + o], m2_rs.at[core, piece], x_peer[o])

    def to_core(piece, ss):
        ref = m_all.at[core, piece]
        send(ref, ref, m3_ss.at[ss], m2_rs.at[core, piece], core_pair)

    share(k, 0, True)
    to_core(k, 0)

    arrived(w_all.at[1 - b], w_rs)

    def stage_a(offset):
        for side, dst in ((1 - core, p_send), (core, p_own)):

            @pl.loop(0, 2)
            def _(t):
                rows = pl.ds(pl.multiple_of(t * 256, 256), 256)
                total = dot_nt(c_src(offset, 0)[rows, :], w_all[side, 0])
                total += dot_nt(c_src(offset, 1)[rows, :], w_all[side, 1])
                dst[offset, rows, :] = total

            if dst is p_send:
                send(p_send.at[offset], p_recv.at[offset], p_ss.at[offset], p_rs.at[offset], core_pair)

    def stage_b(offset):
        arrived(p_recv.at[offset], p_rs.at[offset])
        p_own[offset] += p_recv[offset]
        for o in (2, 1, 3):
            rows = pl.ds(pl.multiple_of(xs[o] * 128, 128), 128)
            send(
                p_own.at[offset, rows, :], x_recv.at[offset, o - 1],
                x_ss.at[offset, o - 1], x_rs.at[offset, o - 1], x_peer[o],
            )

    def stage_c(offset):
        for o in (1, 3, 2):
            arrived(x_recv.at[offset, o - 1], x_rs.at[offset, o - 1])
        total = p_own[offset, pl.ds(pl.multiple_of(x * 128, 128), 128), :]
        for o in (1, 3, 2):
            total += x_recv[offset, o - 1]
        s_own[offset] = total
        half = pl.ds(pl.multiple_of((1 - h) * 64, 64), 64)
        send(s_own.at[offset, half, :], y_recv.at[offset], y_ss.at[offset], y_rs.at[offset], h_pair)

    finals = []

    def stage_d(offset):
        arrived(y_recv.at[offset], y_rs.at[offset])
        total = s_own[offset, pl.ds(pl.multiple_of(h * 64, 64), 64), :] + y_recv[offset]
        o_send[offset] = total.astype(jnp.bfloat16)
        copy = pltpu.make_async_remote_copy(
            src_ref=o_send.at[offset], dst_ref=mg_ref.at[k], send_sem=o_ss.at[offset], recv_sem=o_rs.at[k],
            device_id=line_peer[offset], device_id_type=MESH,
        )
        if offset == 0:
            own = pltpu.make_async_copy(o_send.at[0], mg_ref.at[k], o_rs.at[k])
            pl.when(diagonal)(own.start)
            pl.when(jnp.logical_not(diagonal))(copy.start)
        else:
            copy.start()
        finals.append(copy)

    def weight(offset, first):
        for side in range(2):
            m_t = m_all[side, :, offset].reshape(512, 256).T
            for l in range(2):
                term = jnp.dot(m_t, c_src(offset, l)[...], preferred_element_type=F32)
                if first:
                    acc[l, side] = term
                else:
                    acc[l, side] += term

    stage_a(0)
    c_wait(1, 0)
    c_step(2, 0)
    arrived(m_all.at[core, kh], m2_rs.at[core, kh])
    share(kh, 4, False)
    to_core(kh, 1)
    stage_b(0)
    c_wait(1, 1)
    c_step(2, 1)
    stage_a(7)
    stage_a(1)
    stage_c(0)
    stage_b(7)
    stage_b(1)
    c_wait(2, 0)
    c_step(3, 0)
    n = 2
    for o in (1, 3, 2):
        for t in range(2):
            piece = xs[o] * 2 + t
            arrived(m_all.at[core, piece], m2_rs.at[core, piece])
            to_core(piece, n)
            n += 1
    stage_d(0)
    stage_c(7)
    stage_c(1)
    c_wait(2, 1)
    c_step(3, 1)
    stage_a(6)
    stage_a(2)
    stage_d(7)
    stage_d(1)
    for t in range(8):
        arrived(m_all.at[1 - core, t], m2_rs.at[1 - core, t])
    weight(0, True)
    stage_b(6)
    stage_b(2)
    c_wait(3, 0)
    c_step(4, 0)
    weight(7, False)
    stage_c(6)
    stage_c(2)
    weight(1, False)
    c_wait(3, 1)
    c_step(4, 1)
    stage_a(5)
    stage_a(3)
    weight(6, False)
    stage_b(5)
    stage_b(3)
    stage_d(6)
    stage_d(2)
    weight(2, False)
    weight(5, False)
    weight(3, False)
    c_wait(4, 0)
    c_wait(4, 1)
    stage_a(4)
    weight(4, False)
    for l in range(2):
        send(acc.at[l, 1 - b], wg_recv.at[l], g_ss.at[l], g_rs.at[l], y_pair)
    stage_b(4)
    stage_c(5)
    stage_c(3)
    stage_d(5)
    stage_d(3)
    stage_c(4)
    stage_d(4)
    for l in range(2):
        arrived(wg_recv.at[l], g_rs.at[l])
        wg_ref[l] = acc[l, b] + wg_recv[l]
    for t in range(8):
        arrived(mg_ref.at[t], o_rs.at[t])

    for copy in sent:
        copy.wait_send()
    for copies in (m1, finals):
        pl.when(jnp.logical_not(diagonal))(copies[0].wait_send)
        for copy in copies[1:]:
            copy.wait_send()


def on_device(memory, joined_weight, joined_cotangent):
    dma = pltpu.SemaphoreType.DMA
    bf16 = jnp.bfloat16
    memory_grad, weight_grad = pl.pallas_call(
        kernel,
        out_shape=(
            jax.ShapeDtypeStruct((8, 64, 256), bf16),
            jax.ShapeDtypeStruct((2, 256, 512), F32),
        ),
        in_specs=[pl.BlockSpec(memory_space=pltpu.VMEM)] * 3,
        out_specs=(pl.BlockSpec(memory_space=pltpu.VMEM),) * 2,
        scratch_shapes=[
            pltpu.VMEM((8, 2, 512, 512), bf16),
            pltpu.VMEM((2, 2, 256, 512), bf16),
            pltpu.VMEM((2, 8, 8, 64, 256), bf16),
            pltpu.VMEM((8, 512, 256), F32),
            pltpu.VMEM((8, 512, 256), F32),
            pltpu.VMEM((8, 512, 256), F32),
            pltpu.VMEM((8, 3, 128, 256), F32),
            pltpu.VMEM((8, 128, 256), F32),
            pltpu.VMEM((8, 64, 256), F32),
            pltpu.VMEM((8, 64, 256), bf16),
            pltpu.VMEM((2, 2, 256, 512), F32),
            pltpu.VMEM((2, 256, 512), F32),
            dma((2, 4, 2)), dma((2, 4, 2)),
            dma, dma,
            dma((8,)), dma((8,)),
            dma((8,)), dma((2, 8)), dma((8,)),
            dma((8,)), dma((8,)),
            dma((8, 3)), dma((8, 3)),
            dma((8,)), dma((8,)),
            dma((8,)), dma((8,)),
            dma((2,)), dma((2,)),
        ],
        compiler_params=pltpu.CompilerParams(
            collective_id=0, has_side_effects=True, vmem_limit_bytes=52 * 1024 * 1024
        ),
    )(memory, joined_weight, joined_cotangent)
    return memory_grad.reshape(512, 256), weight_grad


def solution(mesh):
    in_specs = (P("row", "col"), P(None, "row", "col"), P(None, "row", "col"))
    out_specs = (P("row", "col"), P(None, "row", "col"))
    return jax.shard_map(
        on_device, mesh=mesh, in_specs=in_specs, out_specs=out_specs, check_vma=False
    )
```

time: 757 us -> 163 us (0.22)
  waiting for transfers between devices: 711 us -> 0 us
  Pallas kernels: 0 us -> 158 us
  matrix products: 25.8 us -> 0 us
  between operations: 13.8 us -> 0.65 us
    reduce_scatter x3 -> x0, waiting for transfers between devices: 474 us -> none  [the longest x2 362 us: on_device(): lax.psum_scatter(term_fn(jnp.int32(0), joined_weight.shape[1] * lax.axis_...]
    all_gather x2 -> x0, waiting for transfers between devices: 236 us -> none  [the longest x1 169 us: on_device(): lax.all_gather(joined_weight, 'row', axis=1, tiled=True)]
    pallas_call x0 -> x1, Pallas kernels: none -> 158 us  [on_device(): pl.pallas_call(kernel, out_shape=(jax.ShapeDtypeStruct((8, 64, 256), bf16...]
    dot_general x3 -> x0, matrix products: 25.8 us -> none  [the longest x2 15.7 us: layer_term(): lax.dot_general(memory_row, cotangent, (((0,), (0,)), ((), ())), preferre...]
  transfers between devices with their start and end apart: 5 -> 0, of which waited for: 5 -> 0; matrix products, arithmetic and copies ran while one was open for 4% -> 0% of each run, Pallas kernels for 0% -> 0%
where the time goes in v1:
time: 163 us
  Pallas kernels  158 us (97%)
  local copies, waits for them, and re-layouts  4.95 us (3%)
    pallas_call x1, Pallas kernels, on_device(): pl.pallas_call(kernel, out_shape=(jax.ShapeDtypeStruct((8, 64, 256), bf16...  158 us
    unnamed x6, local copies, waits for them, and re-layouts  4.95 us

profile of v1, /device:TPU:4, one launch (start us, length us, event | category | flops | bytes accessed | tf_op | source)
XLA Modules:
  0.0 163.3 jit_solution(7959029674571100059)
XLA Ops:
  0.6 0.0 copy-start
  0.6 1.0 copy-done
  1.7 0.0 copy-start.1
  1.7 0.9 copy-done.1
  2.6 157.7 %shard_map.50 = (bf16[8,64,256]{2,1,0:T(8,128)(2,1)S(1)}, f32[2,256,512]{2,1,0:T(8,128)}) custom-call(bf16[512,256]{1,0:T(8,128)(2,1)S(1)} %copy-done.1, bf16[2,256,512]{2,1,0:T(8,128)(2,1)S(1)} %copy-done, bf16[2,512,512]{2,1,0:T(8,128)(2,1)} %c_ref.1), custom_call_target="tpu_custom_call" | custom-call | tf_op jit(solution)/shard_map/pallas_call | solution.py:267
  160.3 0.7 copy.7
  161.0 2.3 %copy.8 = f32[2,256,512]{2,1,0:T(8,128)} copy(f32[2,256,512]{2,1,0:T(8,128)} %get-tuple-element.9) | data formatting | bytes 2097152
Async XLA Ops:
  0.6 1.0 copy-start
  1.7 0.9 copy-start.1

commit v2 on v0

v2 whole, which is shorter than its diff:
```python
import jax
import jax.numpy as jnp
from jax import lax
from jax.experimental import pallas as pl
from jax.experimental.pallas import tpu as pltpu
from jax.sharding import PartitionSpec as P

MESH = pl.DeviceIdType.MESH
F32 = jnp.float32
H_FIRST = (1, 2, 3)


def dot_nt(a, b):
    return lax.dot_general(a, b, (((1,), (1,)), ((), ())), preferred_element_type=F32)


def kernel(
    m_ref, w_ref, c_ref, mg_ref, wg_ref,
    c_all, w_all, m_a, m_all, p_own, p_send, p_recv, x_recv, s_own, y_recv, h_recv, h_own, v_recv,
    o_send, acc, wg_recv,
    in_s, c_ss, c_rs, w_ss, w_rs, ma_ss, ma_rs, mb_ss, mb_rs, m2_ss, m2_rs, m3_ss, p_ss, p_rs,
    x_ss, x_rs, y_ss, y_rs, h_ss, h_rs, v_ss, v_rs, o_ss, o_rs, g_ss, g_rs,
):
    row, col = lax.axis_index("row"), lax.axis_index("col")
    z, b = lax.div(row, 2), lax.rem(row, 2)
    k, core = lax.div(col, 2), lax.rem(col, 2)
    x, h = lax.div(k, 2), lax.rem(k, 2)
    ks = [lax.rem(k + o, 8) for o in range(8)]
    zs = [lax.rem(z + o, 8) for o in range(8)]
    xs = [lax.rem(x + o, 4) for o in range(4)]
    plane = [(row, ks[o] * 2 + core) for o in range(8)]
    line = [(zs[o] * 2 + b, col) for o in range(8)]
    up, down = line[1], line[7]
    y_pair = (z * 2 + 1 - b, col)
    core_pair = (row, k * 2 + 1 - core)
    h_pair = (row, (x * 2 + 1 - h) * 2 + core)
    x_peer = [(row, (xs[o] * 2 + h) * 2 + core) for o in range(4)]
    home = [(zs[o] * 2 + b, z * 2 + core) for o in range(8)]
    at_home = z == k

    c_in = pltpu.make_async_copy(c_ref, c_all.at[0], in_s.at[0])
    w_in = pltpu.make_async_copy(w_ref, w_all.at[b], in_s.at[1])
    c_in.start()
    w_in.start()

    barrier = pltpu.get_barrier_semaphore()
    greeted = plane[1:] + line[1:] + [y_pair, core_pair]
    for peer in greeted:
        pl.semaphore_signal(barrier, inc=1, device_id=peer, device_id_type=MESH)
    pl.semaphore_wait(barrier, len(greeted))

    sent = []

    def send(src, dst, ss, rs, peer):
        copy = pltpu.make_async_remote_copy(
            src_ref=src, dst_ref=dst, send_sem=ss, recv_sem=rs, device_id=peer, device_id_type=MESH
        )
        copy.start()
        sent.append(copy)

    def arrived(dst, rs):
        pltpu.make_async_copy(dst, dst, rs).wait()

    def part(offset, l, r):
        return c_all.at[offset, l, pl.ds(r * 256, 256), :]

    def c_step(step, l, r):
        mine = c_ref.at[l, pl.ds(r * 256, 256), :]
        if step < 4 or r == 0:
            src = mine if step == 1 else part(9 - step, l, r)
            send(src, part(8 - step, l, r), c_ss.at[0, step - 1, l, r], c_rs.at[0, step - 1, l, r], up)
        if step < 4 or r == 1:
            src = mine if step == 1 else part(step - 1, l, r)
            send(src, part(step, l, r), c_ss.at[1, step - 1, l, r], c_rs.at[1, step - 1, l, r], down)

    def c_wait(step, l, r):
        if step < 4 or r == 0:
            arrived(part(8 - step, l, r), c_rs.at[0, step - 1, l, r])
        if step < 4 or r == 1:
            arrived(part(step, l, r), c_rs.at[1, step - 1, l, r])

    def c_next(step, l):
        for r in range(2):
            c_wait(step, l, r)
            if step < 4:
                c_step(step + 1, l, r)

    c_step(1, 0, 0)
    c_step(1, 0, 1)

    def m_rows(j):
        return m_ref.at[pl.ds(pl.multiple_of(j * 64, 64), 64), :]

    for o in range(1, 8):
        send(m_rows(ks[o]), m_a.at[k], ma_ss.at[o], ma_rs.at[k], plane[o])
    m_in = pltpu.make_async_copy(m_rows(k), m_a.at[k], ma_rs.at[k])
    m_in.start()
    send(w_ref, w_all.at[b], w_ss, w_rs, y_pair)

    for o in (4, 3, 5, 2, 6, 1, 7, 0):
        piece = m_a.at[zs[o]]
        arrived(piece, ma_rs.at[zs[o]])
        slot = (8 - o) % 8
        if o:
            send(piece, m_all.at[core, k, slot], mb_ss.at[o], mb_rs.at[slot], line[o])
        else:
            pltpu.make_async_copy(piece, m_all.at[core, k, 0], mb_rs.at[0]).start()

    kh = x * 2 + 1 - h

    def share(piece, n, to_h):
        ref = m_all.at[core, piece]
        if to_h:
            send(ref, ref, m2_ss.at[n], m2_rs.at[core, piece], h_pair)
        for o in (1, 3, 2):
            send(ref, ref, m2_ss.at[n + o], m2_rs.at[core, piece], x_peer[o])

    def to_core(piece, n):
        ref = m_all.at[core, piece]
        send(ref, ref, m3_ss.at[n], m2_rs.at[core, piece], core_pair)

    def got(side, piece):
        arrived(m_all.at[side, piece], m2_rs.at[side, piece])

    def partial(offset):
        for side, dst in ((1 - core, p_send), (core, p_own)):

            @pl.loop(0, 2)
            def _(t):
                rows = pl.ds(pl.multiple_of(t * 256, 256), 256)
                total = dot_nt(c_all[offset, 0, rows, :], w_all[side, 0])
                total += dot_nt(c_all[offset, 1, rows, :], w_all[side, 1])
                dst[offset, pl.ds(t * 2, 2)] = total.reshape(2, 2, 64, 256)

            if dst is p_send:
                send(p_send.at[offset], p_recv.at[offset], p_ss.at[offset], p_rs.at[offset], core_pair)

    def scatter(offset):
        arrived(p_recv.at[offset], p_rs.at[offset])
        p_own[offset] += p_recv[offset]
        if offset in H_FIRST:
            n = H_FIRST.index(offset)
            send(p_own.at[offset, :, 1 - h], h_recv.at[n], h_ss.at[n], h_rs.at[n], h_pair)
            return
        for o in (2, 1, 3):
            send(
                p_own.at[offset, xs[o]], x_recv.at[offset, o - 1],
                x_ss.at[offset, o - 1], x_rs.at[offset, o - 1], x_peer[o],
            )

    def scatter_more(offset):
        if offset in H_FIRST:
            n = H_FIRST.index(offset)
            arrived(h_recv.at[n], h_rs.at[n])
            h_own[n] = p_own[offset, :, h] + h_recv[n]
            for o in (2, 1, 3):
                send(
                    h_own.at[n, xs[o]], v_recv.at[n, o - 1],
                    v_ss.at[n, o - 1], v_rs.at[n, o - 1], x_peer[o],
                )
            return
        for o in (1, 3, 2):
            arrived(x_recv.at[offset, o - 1], x_rs.at[offset, o - 1])
        total = p_own[offset, x]
        for o in (1, 3, 2):
            total += x_recv[offset, o - 1]
        s_own[offset] = total
        send(s_own.at[offset, 1 - h], y_recv.at[offset], y_ss.at[offset], y_rs.at[offset], h_pair)

    def finish(offset):
        if offset in H_FIRST:
            n = H_FIRST.index(offset)
            for o in (1, 3, 2):
                arrived(v_recv.at[n, o - 1], v_rs.at[n, o - 1])
            total = h_own[n, x]
            for o in (1, 3, 2):
                total += v_recv[n, o - 1]
        else:
            arrived(y_recv.at[offset], y_rs.at[offset])
            total = s_own[offset, h] + y_recv[offset]
        o_send[offset] = total.astype(jnp.bfloat16)

    finals = {}

    def deliver(offset):
        copy = pltpu.make_async_remote_copy(
            src_ref=o_send.at[offset], dst_ref=mg_ref.at[k], send_sem=o_ss.at[offset], recv_sem=o_rs.at[k],
            device_id=home[offset], device_id_type=MESH,
        )
        if offset == 0:
            own = pltpu.make_async_copy(o_send.at[0], mg_ref.at[k], o_rs.at[k])
            pl.when(at_home)(own.start)
            pl.when(jnp.logical_not(at_home))(copy.start)
        else:
            copy.start()
        finals[offset] = copy

    def weight(l, side, offset):
        m_t = m_all[side, :, offset].reshape(512, 256).T
        term = jnp.dot(m_t, c_all[offset, l], preferred_element_type=F32)
        if offset == 0:
            acc[l, side] = term
        else:
            acc[l, side] += term

    def weight_send(l):
        send(acc.at[l, 1 - b], wg_recv.at[l], g_ss.at[l], g_rs.at[l], y_pair)

    def weight_end(l):
        arrived(wg_recv.at[l], g_rs.at[l])
        wg_ref[l] = acc[l, b] + wg_recv[l]

    w_in.wait()
    c_in.wait()
    arrived(w_all.at[1 - b], w_rs)
    partial(0)
    c_next(1, 0)
    for o in range(8):
        arrived(m_all.at[core, k, o], mb_rs.at[o])
    share(k, 0, True)
    to_core(k, 0)
    scatter(0)
    got(core, kh)
    share(kh, 4, False)
    to_core(kh, 1)
    c_next(2, 0)
    scatter_more(0)
    c_next(3, 0)
    c_step(1, 1, 0)
    c_step(1, 1, 1)
    n = 2
    for o in (1, 3, 2):
        for t in range(2):
            got(core, xs[o] * 2 + t)
            to_core(xs[o] * 2 + t, n)
            n += 1
    finish(0)
    c_next(4, 0)
    for t in range(8):
        got(1 - core, t)
    for side in (1 - b, b):
        for o in range(8):
            weight(0, side, o)
        if side is not b:
            weight_send(0)
    c_next(1, 1)
    partial(7)
    partial(1)
    for o in (0, 7, 1):
        for side in range(2):
            weight(1, side, o)
    scatter(7)
    scatter(1)
    c_next(2, 1)
    partial(6)
    partial(2)
    scatter_more(7)
    scatter_more(1)
    scatter(6)
    scatter(2)
    for o in (6, 2):
        for side in range(2):
            weight(1, side, o)
    weight_end(0)
    c_next(3, 1)
    partial(5)
    partial(3)
    finish(7)
    finish(1)
    scatter_more(6)
    scatter_more(2)
    scatter(5)
    scatter(3)
    for o in (5, 3):
        for side in range(2):
            weight(1, side, o)
    c_next(4, 1)
    weight(1, 1 - b, 4)
    weight_send(1)
    for o in (0, 7, 1):
        deliver(o)
    partial(4)
    scatter(4)
    finish(6)
    finish(2)
    deliver(6)
    deliver(2)
    weight(1, b, 4)
    scatter_more(5)
    scatter_more(3)
    scatter_more(4)
    for o in (5, 3, 4):
        finish(o)
        deliver(o)
    weight_end(1)
    for t in range(8):
        arrived(mg_ref.at[t], o_rs.at[t])

    for copy in sent:
        copy.wait_send()
    pl.when(jnp.logical_not(at_home))(finals[0].wait_send)
    for o in range(1, 8):
        finals[o].wait_send()


def on_device(memory, joined_weight, joined_cotangent):
    dma = pltpu.SemaphoreType.DMA
    bf16 = jnp.bfloat16
    memory_grad, weight_grad = pl.pallas_call(
        kernel,
        out_shape=(
            jax.ShapeDtypeStruct((8, 64, 256), bf16),
            jax.ShapeDtypeStruct((2, 256, 512), F32),
        ),
        in_specs=[pl.BlockSpec(memory_space=pltpu.HBM)] * 3,
        out_specs=(pl.BlockSpec(memory_space=pltpu.VMEM),) * 2,
        scratch_shapes=[
            pltpu.VMEM((8, 2, 512, 512), bf16),
            pltpu.VMEM((2, 2, 256, 512), bf16),
            pltpu.VMEM((8, 64, 256), bf16),
            pltpu.VMEM((2, 8, 8, 64, 256), bf16),
            pltpu.VMEM((8, 4, 2, 64, 256), F32),
            pltpu.VMEM((8, 4, 2, 64, 256), F32),
            pltpu.VMEM((8, 4, 2, 64, 256), F32),
            pltpu.VMEM((8, 3, 2, 64, 256), F32),
            pltpu.VMEM((8, 2, 64, 256), F32),
            pltpu.VMEM((8, 64, 256), F32),
            pltpu.VMEM((3, 4, 64, 256), F32),
            pltpu.VMEM((3, 4, 64, 256), F32),
            pltpu.VMEM((3, 3, 64, 256), F32),
            pltpu.VMEM((8, 64, 256), bf16),
            pltpu.VMEM((2, 2, 256, 512), F32),
            pltpu.VMEM((2, 256, 512), F32),
            dma((2,)),
            dma((2, 4, 2, 2)), dma((2, 4, 2, 2)),
            dma, dma,
            dma((8,)), dma((8,)),
            dma((8,)), dma((8,)),
            dma((8,)), dma((2, 8)), dma((8,)),
            dma((8,)), dma((8,)),
            dma((8, 3)), dma((8, 3)),
            dma((8,)), dma((8,)),
            dma((3,)), dma((3,)),
            dma((3, 3)), dma((3, 3)),
            dma((8,)), dma((8,)),
            dma((2,)), dma((2,)),
        ],
        compiler_params=pltpu.CompilerParams(
            collective_id=0, has_side_effects=True, vmem_limit_bytes=56 * 1024 * 1024
        ),
    )(memory, joined_weight, joined_cotangent)
    return memory_grad.reshape(512, 256), weight_grad


def solution(mesh):
    in_specs = (P("row", "col"), P(None, "row", "col"), P(None, "row", "col"))
    out_specs = (P("row", "col"), P(None, "row", "col"))
    return jax.shard_map(
        on_device, mesh=mesh, in_specs=in_specs, out_specs=out_specs, check_vma=False
    )
```

time: 757 us -> 136 us (0.18)
  waiting for transfers between devices: 711 us -> 0 us
  Pallas kernels: 0 us -> 131 us
  matrix products: 25.8 us -> 0 us
  between operations: 13.8 us -> 0.64 us
    reduce_scatter x3 -> x0, waiting for transfers between devices: 474 us -> none  [the longest x2 362 us: on_device(): lax.psum_scatter(term_fn(jnp.int32(0), joined_weight.shape[1] * lax.axis_...]
    all_gather x2 -> x0, waiting for transfers between devices: 236 us -> none  [the longest x1 169 us: on_device(): lax.all_gather(joined_weight, 'row', axis=1, tiled=True)]
    pallas_call x0 -> x1, Pallas kernels: none -> 131 us  [on_device(): pl.pallas_call(kernel, out_shape=(jax.ShapeDtypeStruct((8, 64, 256), bf16...]
    dot_general x3 -> x0, matrix products: 25.8 us -> none  [the longest x2 15.7 us: layer_term(): lax.dot_general(memory_row, cotangent, (((0,), (0,)), ((), ())), preferre...]
  transfers between devices with their start and end apart: 5 -> 0, of which waited for: 5 -> 0; matrix products, arithmetic and copies ran while one was open for 4% -> 0% of each run, Pallas kernels for 0% -> 0%
where the time goes in v2:
time: 136 us
  Pallas kernels  131 us (96%)
  local copies, waits for them, and re-layouts  3.93 us (3%)
    pallas_call x1, Pallas kernels, on_device(): pl.pallas_call(kernel, out_shape=(jax.ShapeDtypeStruct((8, 64, 256), bf16...  131 us
    unnamed x2, local copies, waits for them, and re-layouts  3.93 us

profile of v2, /device:TPU:4, one launch (start us, length us, event | category | flops | bytes accessed | tf_op | source)
XLA Modules:
  0.0 135.7 jit_solution(14171175635715604360)
XLA Ops:
  0.6 131.1 %shard_map.50 = (bf16[8,64,256]{2,1,0:T(8,128)(2,1)}, f32[2,256,512]{2,1,0:T(8,128)}) custom-call(bf16[512,256]{1,0:T(8,128)(2,1)} %m_ref.1, bf16[2,256,512]{2,1,0:T(8,128)(2,1)} %w_ref.1, bf16[2,512,512]{2,1,0:T(8,128)(2,1)} %c_ref.1), custom_call_target="tpu_custom_call" | custom-call | tf_op jit(solution)/shard_map/pallas_call | solution.py:309
  131.7 1.7 %copy.7 = bf16[512,256]{1,0:T(8,128)(2,1)} copy(bf16[512,256]{1,0:T(8,128)(2,1)} %bitcast.1) | data formatting | bytes 524288
  133.4 2.3 %copy.8 = f32[2,256,512]{2,1,0:T(8,128)} copy(f32[2,256,512]{2,1,0:T(8,128)} %get-tuple-element.9) | data formatting | bytes 2097152

commit v3 on v2

--- a/solution.py
+++ b/solution.py
@@ -79,14 +79,13 @@
         if step < 4 or r == 1:
             arrived(part(step, l, r), c_rs.at[1, step - 1, l, r])
 
-    def c_next(step, l):
+    def c_next(step, l, onward=True):
         for r in range(2):
             c_wait(step, l, r)
-            if step < 4:
+            if step < 4 and onward:
                 c_step(step + 1, l, r)
 
     c_step(1, 0, 0)
-    c_step(1, 0, 1)
 
     def m_rows(j):
         return m_ref.at[pl.ds(pl.multiple_of(j * 64, 64), 64), :]
@@ -106,6 +105,10 @@
         else:
             pltpu.make_async_copy(piece, m_all.at[core, k, 0], mb_rs.at[0]).start()
 
+    c_step(1, 0, 1)
+    c_step(1, 1, 0)
+    c_step(1, 1, 1)
+
     kh = x * 2 + 1 - h
 
     def share(piece, n, to_h):
@@ -124,14 +127,9 @@
 
     def partial(offset):
         for side, dst in ((1 - core, p_send), (core, p_own)):
-
-            @pl.loop(0, 2)
-            def _(t):
-                rows = pl.ds(pl.multiple_of(t * 256, 256), 256)
-                total = dot_nt(c_all[offset, 0, rows, :], w_all[side, 0])
-                total += dot_nt(c_all[offset, 1, rows, :], w_all[side, 1])
-                dst[offset, pl.ds(t * 2, 2)] = total.reshape(2, 2, 64, 256)
-
+            total = dot_nt(c_all[offset, 0], w_all[side, 0])
+            total += dot_nt(c_all[offset, 1], w_all[side, 1])
+            dst[offset] = total.reshape(4, 2, 64, 256)
             if dst is p_send:
                 send(p_send.at[offset], p_recv.at[offset], p_ss.at[offset], p_rs.at[offset], core_pair)
 
@@ -203,18 +201,45 @@
         else:
             acc[l, side] += term
 
-    def weight_send(l):
-        send(acc.at[l, 1 - b], wg_recv.at[l], g_ss.at[l], g_rs.at[l], y_pair)
+    def weight_send(l, piece):
+        rows = pl.ds(piece * 64, 64)
+        send(acc.at[l, 1 - b, rows, :], wg_recv.at[l, rows, :], g_ss.at[l, piece], g_rs.at[l, piece], y_pair)
 
     def weight_end(l):
-        arrived(wg_recv.at[l], g_rs.at[l])
-        wg_ref[l] = acc[l, b] + wg_recv[l]
+        for piece in range(4):
+            rows = pl.ds(piece * 64, 64)
+            arrived(wg_recv.at[l, rows, :], g_rs.at[l, piece])
+            wg_ref[l, rows, :] = acc[l, b, rows, :] + wg_recv[l, rows, :]
+
+    def weights(l, offsets):
+        for side in (1 - b, b):
+            for o in offsets:
+                weight(l, side, o)
+
+    drained = [0]
+
+    def drain(upto):
+        for copy in sent[drained[0]:upto]:
+            copy.wait_send()
+        drained[0] = upto
+
+    def weights(l, offsets):
+        for side in (1 - b, b):
+            for o in offsets:
+                weight(l, side, o)
+
+    drained = [0]
+
+    def drain(upto):
+        for copy in sent[drained[0]:upto]:
+            copy.wait_send()
+        drained[0] = upto
 
     w_in.wait()
     c_in.wait()
+    c_next(1, 0)
     arrived(w_all.at[1 - b], w_rs)
     partial(0)
-    c_next(1, 0)
     for o in range(8):
         arrived(m_all.at[core, k, o], mb_rs.at[o])
     share(k, 0, True)
@@ -223,81 +248,79 @@
     got(core, kh)
     share(kh, 4, False)
     to_core(kh, 1)
-    c_next(2, 0)
-    scatter_more(0)
-    c_next(3, 0)
-    c_step(1, 1, 0)
-    c_step(1, 1, 1)
-    n = 2
-    for o in (1, 3, 2):
-        for t in range(2):
-            got(core, xs[o] * 2 + t)
-            to_core(xs[o] * 2 + t, n)
-            n += 1
-    finish(0)
-    c_next(4, 0)
-    for t in range(8):
-        got(1 - core, t)
-    for side in (1 - b, b):
-        for o in range(8):
-            weight(0, side, o)
-        if side is not b:
-            weight_send(0)
     c_next(1, 1)
     partial(7)
     partial(1)
-    for o in (0, 7, 1):
-        for side in range(2):
-            weight(1, side, o)
     scatter(7)
     scatter(1)
-    c_next(2, 1)
+    c_next(2, 0)
+    n = 2
+    for o in (1, 3, 2):
+        got(core, xs[o] * 2 + h)
+        to_core(xs[o] * 2 + h, n)
+        n += 1
+    scatter_more(0)
+    c_next(2, 1, False)
+    early = len(sent)
     partial(6)
     partial(2)
-    scatter_more(7)
-    scatter_more(1)
+    for o in (1, 3, 2):
+        got(core, xs[o] * 2 + 1 - h)
+        to_core(xs[o] * 2 + 1 - h, n)
+        n += 1
     scatter(6)
     scatter(2)
-    for o in (6, 2):
-        for side in range(2):
-            weight(1, side, o)
-    weight_end(0)
-    c_next(3, 1)
-    partial(5)
-    partial(3)
-    finish(7)
-    finish(1)
+    finish(0)
+    scatter_more(1)
+    for t in range(8):
+        got(1 - core, t)
+    weights(0, (0, 7, 1, 6, 2))
+    weights(1, (0, 7, 1, 6, 2))
+    c_next(3, 0)
+    c_step(3, 1, 0)
+    c_step(3, 1, 1)
+    scatter_more(7)
+    weights(0, (5, 3))
     scatter_more(6)
     scatter_more(2)
+    drain(early)
+    c_next(4, 0)
+    weight(0, 1 - b, 4)
+    for piece in range(4):
+        weight_send(0, piece)
+    weight(0, b, 4)
+    for o in (7, 1, 6, 2):
+        finish(o)
+    early = len(sent)
+    c_next(3, 1)
+    for o in (0, 7, 1, 6, 2):
+        deliver(o)
+    partial(3)
+    partial(5)
+    scatter(3)
     scatter(5)
-    scatter(3)
-    for o in (5, 3):
-        for side in range(2):
-            weight(1, side, o)
+    weights(1, (5, 3))
+    drain(early)
+    weight_end(0)
     c_next(4, 1)
+    partial(4)
     weight(1, 1 - b, 4)
-    weight_send(1)
-    for o in (0, 7, 1):
-        deliver(o)
-    partial(4)
+    weight_send(1, 0)
+    weight_send(1, 1)
     scatter(4)
-    finish(6)
-    finish(2)
-    deliver(6)
-    deliver(2)
     weight(1, b, 4)
     scatter_more(5)
     scatter_more(3)
+    weight_send(1, 2)
     scatter_more(4)
+    weight_send(1, 3)
     for o in (5, 3, 4):
         finish(o)
         deliver(o)
     weight_end(1)
     for t in range(8):
         arrived(mg_ref.at[t], o_rs.at[t])
-
-    for copy in sent:
-        copy.wait_send()
+    drain(len(sent))
     pl.when(jnp.logical_not(at_home))(finals[0].wait_send)
     for o in range(1, 8):
         finals[o].wait_send()
@@ -343,7 +366,7 @@
             dma((3,)), dma((3,)),
             dma((3, 3)), dma((3, 3)),
             dma((8,)), dma((8,)),
-            dma((2,)), dma((2,)),
+            dma((2, 4)), dma((2, 4)),
         ],
         compiler_params=pltpu.CompilerParams(
             collective_id=0, has_side_effects=True, vmem_limit_bytes=56 * 1024 * 1024

time: 136 us -> 130 us (0.956)
  Pallas kernels: 131 us -> 125 us
    pallas_call x1, Pallas kernels: 131 us -> 125 us  [on_device(): pl.pallas_call(kernel, out_shape=(jax.ShapeDtypeStruct((8, 64, 256), bf16...]
where the time goes in v3:
time: 130 us
  Pallas kernels  125 us (96%)
  local copies, waits for them, and re-layouts  3.93 us (3%)
    pallas_call x1, Pallas kernels, on_device(): pl.pallas_call(kernel, out_shape=(jax.ShapeDtypeStruct((8, 64, 256), bf16...  125 us
    unnamed x2, local copies, waits for them, and re-layouts  3.93 us

profile of v3, /device:TPU:4, one launch (start us, length us, event | category | flops | bytes accessed | tf_op | source)
XLA Modules:
  0.0 129.9 jit_solution(17033035815977639043)
XLA Ops:
  0.6 125.4 %shard_map.50 = (bf16[8,64,256]{2,1,0:T(8,128)(2,1)}, f32[2,256,512]{2,1,0:T(8,128)}) custom-call(bf16[512,256]{1,0:T(8,128)(2,1)} %m_ref.1, bf16[2,256,512]{2,1,0:T(8,128)(2,1)} %w_ref.1, bf16[2,512,512]{2,1,0:T(8,128)(2,1)} %c_ref.1), custom_call_target="tpu_custom_call" | custom-call | tf_op jit(solution)/shard_map/pallas_call | solution.py:332
  126.0 1.7 %copy.7 = bf16[512,256]{1,0:T(8,128)(2,1)} copy(bf16[512,256]{1,0:T(8,128)(2,1)} %bitcast.1) | data formatting | bytes 524288
  127.7 2.3 %copy.8 = f32[2,256,512]{2,1,0:T(8,128)} copy(f32[2,256,512]{2,1,0:T(8,128)} %get-tuple-element.9) | data formatting | bytes 2097152

commit v4 on v3

--- a/solution.py
+++ b/solution.py
@@ -15,7 +15,7 @@
 
 
 def kernel(
-    m_ref, w_ref, c_ref, mg_ref, wg_ref,
+    m_ref, w_ref, c_ref, mg_ref, wg_ref, wg_sum, wg_s,
     c_all, w_all, m_a, m_all, p_own, p_send, p_recv, x_recv, s_own, y_recv, h_recv, h_own, v_recv,
     o_send, acc, wg_recv,
     in_s, c_ss, c_rs, w_ss, w_rs, ma_ss, ma_rs, mb_ss, mb_rs, m2_ss, m2_rs, m3_ss, p_ss, p_rs,
@@ -62,10 +62,10 @@
         pltpu.make_async_copy(dst, dst, rs).wait()
 
     def part(offset, l, r):
-        return c_all.at[offset, l, pl.ds(r * 256, 256), :]
+        return c_all.at[offset, l, pl.ds(r * 2, 2)]
 
     def c_step(step, l, r):
-        mine = c_ref.at[l, pl.ds(r * 256, 256), :]
+        mine = c_ref.at[l, pl.ds(r * 2, 2)]
         if step < 4 or r == 0:
             src = mine if step == 1 else part(9 - step, l, r)
             send(src, part(8 - step, l, r), c_ss.at[0, step - 1, l, r], c_rs.at[0, step - 1, l, r], up)
@@ -84,6 +84,27 @@
             c_wait(step, l, r)
             if step < 4 and onward:
                 c_step(step + 1, l, r)
+
+    def batch(offset, t, f):
+        return c_all.at[offset, 1, :, :, t, :, pl.ds(f * 256, 256)]
+
+    def third_send(t, f):
+        g = 1 - f
+        send(batch(6, t, f), batch(5, t, f), c_ss.at[0, 2, 1, 2 * t + f], c_rs.at[0, 2, 1, 2 * t + f], up)
+        send(batch(2, t, g), batch(3, t, g), c_ss.at[1, 2, 1, 2 * t + g], c_rs.at[1, 2, 1, 2 * t + g], down)
+
+    def third_wait(t, f):
+        g = 1 - f
+        arrived(batch(5, t, f), c_rs.at[0, 2, 1, 2 * t + f])
+        arrived(batch(3, t, g), c_rs.at[1, 2, 1, 2 * t + g])
+
+    def fourth_send(t):
+        send(batch(5, t, 0), batch(4, t, 0), c_ss.at[0, 3, 1, t], c_rs.at[0, 3, 1, t], up)
+        send(batch(3, t, 1), batch(4, t, 1), c_ss.at[1, 3, 1, t], c_rs.at[1, 3, 1, t], down)
+
+    def fourth_wait(t):
+        arrived(batch(4, t, 0), c_rs.at[0, 3, 1, t])
+        arrived(batch(4, t, 1), c_rs.at[1, 3, 1, t])
 
     c_step(1, 0, 0)
 
@@ -125,77 +146,90 @@
     def got(side, piece):
         arrived(m_all.at[side, piece], m2_rs.at[side, piece])
 
-    def partial(offset):
+    def rows_of(t):
+        return slice(None) if t is None else t
+
+    def partial(offset, t=None):
+        at, n = rows_of(t), t or 0
         for side, dst in ((1 - core, p_send), (core, p_own)):
-            total = dot_nt(c_all[offset, 0], w_all[side, 0])
-            total += dot_nt(c_all[offset, 1], w_all[side, 1])
-            dst[offset] = total.reshape(4, 2, 64, 256)
+            total = dot_nt(c_all[offset, 0, :, :, at].reshape(-1, 512), w_all[side, 0])
+            total += dot_nt(c_all[offset, 1, :, :, at].reshape(-1, 512), w_all[side, 1])
+            shape = (4, 2, 2, 32, 256) if t is None else (4, 2, 32, 256)
+            dst[offset, :, :, at] = total.reshape(shape)
             if dst is p_send:
-                send(p_send.at[offset], p_recv.at[offset], p_ss.at[offset], p_rs.at[offset], core_pair)
-
-    def scatter(offset):
-        arrived(p_recv.at[offset], p_rs.at[offset])
-        p_own[offset] += p_recv[offset]
+                send(
+                    p_send.at[offset, :, :, at], p_recv.at[offset, :, :, at],
+                    p_ss.at[offset, n], p_rs.at[offset, n], core_pair,
+                )
+
+    def scatter(offset, t=None):
+        at, n = rows_of(t), t or 0
+        arrived(p_recv.at[offset, :, :, at], p_rs.at[offset, n])
+        p_own[offset, :, :, at] += p_recv[offset, :, :, at]
         if offset in H_FIRST:
-            n = H_FIRST.index(offset)
-            send(p_own.at[offset, :, 1 - h], h_recv.at[n], h_ss.at[n], h_rs.at[n], h_pair)
+            i = H_FIRST.index(offset)
+            send(p_own.at[offset, :, 1 - h, at], h_recv.at[i, :, at], h_ss.at[i, n], h_rs.at[i, n], h_pair)
             return
         for o in (2, 1, 3):
             send(
-                p_own.at[offset, xs[o]], x_recv.at[offset, o - 1],
-                x_ss.at[offset, o - 1], x_rs.at[offset, o - 1], x_peer[o],
+                p_own.at[offset, xs[o], :, at], x_recv.at[offset, o - 1, :, at],
+                x_ss.at[offset, o - 1, n], x_rs.at[offset, o - 1, n], x_peer[o],
             )
 
-    def scatter_more(offset):
+    def scatter_more(offset, t=None):
+        at, n = rows_of(t), t or 0
         if offset in H_FIRST:
-            n = H_FIRST.index(offset)
-            arrived(h_recv.at[n], h_rs.at[n])
-            h_own[n] = p_own[offset, :, h] + h_recv[n]
+            i = H_FIRST.index(offset)
+            arrived(h_recv.at[i, :, at], h_rs.at[i, n])
+            h_own[i, :, at] = p_own[offset, :, h, at] + h_recv[i, :, at]
             for o in (2, 1, 3):
                 send(
-                    h_own.at[n, xs[o]], v_recv.at[n, o - 1],
-                    v_ss.at[n, o - 1], v_rs.at[n, o - 1], x_peer[o],
+                    h_own.at[i, xs[o], at], v_recv.at[i, o - 1, at],
+                    v_ss.at[i, o - 1, n], v_rs.at[i, o - 1, n], x_peer[o],
                 )
             return
         for o in (1, 3, 2):
-            arrived(x_recv.at[offset, o - 1], x_rs.at[offset, o - 1])
-        total = p_own[offset, x]
+            arrived(x_recv.at[offset, o - 1, :, at], x_rs.at[offset, o - 1, n])
+        total = p_own[offset, x, :, at]
         for o in (1, 3, 2):
-            total += x_recv[offset, o - 1]
-        s_own[offset] = total
-        send(s_own.at[offset, 1 - h], y_recv.at[offset], y_ss.at[offset], y_rs.at[offset], h_pair)
-
-    def finish(offset):
+            total += x_recv[offset, o - 1, :, at]
+        s_own[offset, :, at] = total
+        send(s_own.at[offset, 1 - h, at], y_recv.at[offset, at], y_ss.at[offset, n], y_rs.at[offset, n], h_pair)
+
+    def finish(offset, t=None):
+        at, n = rows_of(t), t or 0
         if offset in H_FIRST:
-            n = H_FIRST.index(offset)
+            i = H_FIRST.index(offset)
             for o in (1, 3, 2):
-                arrived(v_recv.at[n, o - 1], v_rs.at[n, o - 1])
-            total = h_own[n, x]
+                arrived(v_recv.at[i, o - 1, at], v_rs.at[i, o - 1, n])
+            total = h_own[i, x, at]
             for o in (1, 3, 2):
-                total += v_recv[n, o - 1]
+                total += v_recv[i, o - 1, at]
         else:
-            arrived(y_recv.at[offset], y_rs.at[offset])
-            total = s_own[offset, h] + y_recv[offset]
-        o_send[offset] = total.astype(jnp.bfloat16)
+            arrived(y_recv.at[offset, at], y_rs.at[offset, n])
+            total = s_own[offset, h, at] + y_recv[offset, at]
+        o_send[offset, at] = total.astype(jnp.bfloat16)
 
     finals = {}
 
-    def deliver(offset):
+    def deliver(offset, t=None):
+        at, n = rows_of(t), t or 0
+        src, dst, rs = o_send.at[offset, at], mg_ref.at[k, at], o_rs.at[k, n]
         copy = pltpu.make_async_remote_copy(
-            src_ref=o_send.at[offset], dst_ref=mg_ref.at[k], send_sem=o_ss.at[offset], recv_sem=o_rs.at[k],
+            src_ref=src, dst_ref=dst, send_sem=o_ss.at[offset, n], recv_sem=rs,
             device_id=home[offset], device_id_type=MESH,
         )
         if offset == 0:
-            own = pltpu.make_async_copy(o_send.at[0], mg_ref.at[k], o_rs.at[k])
+            own = pltpu.make_async_copy(src, dst, rs)
             pl.when(at_home)(own.start)
             pl.when(jnp.logical_not(at_home))(copy.start)
         else:
             copy.start()
-        finals[offset] = copy
+        finals[offset, n] = copy
 
     def weight(l, side, offset):
         m_t = m_all[side, :, offset].reshape(512, 256).T
-        term = jnp.dot(m_t, c_all[offset, l], preferred_element_type=F32)
+        term = jnp.dot(m_t, c_all[offset, l].reshape(512, 512), preferred_element_type=F32)
         if offset == 0:
             acc[l, side] = term
         else:
@@ -205,11 +239,16 @@
         rows = pl.ds(piece * 64, 64)
         send(acc.at[l, 1 - b, rows, :], wg_recv.at[l, rows, :], g_ss.at[l, piece], g_rs.at[l, piece], y_pair)
 
+    results = []
+
     def weight_end(l):
         for piece in range(4):
             rows = pl.ds(piece * 64, 64)
             arrived(wg_recv.at[l, rows, :], g_rs.at[l, piece])
-            wg_ref[l, rows, :] = acc[l, b, rows, :] + wg_recv[l, rows, :]
+            wg_sum[l, rows, :] = acc[l, b, rows, :] + wg_recv[l, rows, :]
+            copy = pltpu.make_async_copy(wg_sum.at[l, rows, :], wg_ref.at[l, rows, :], wg_s.at[l, piece])
+            copy.start()
+            results.append(copy)
 
     def weights(l, offsets):
         for side in (1 - b, b):
@@ -277,8 +316,9 @@
     weights(0, (0, 7, 1, 6, 2))
     weights(1, (0, 7, 1, 6, 2))
     c_next(3, 0)
-    c_step(3, 1, 0)
-    c_step(3, 1, 1)
+    third_send(0, 0)
+    third_send(0, 1)
+    third_send(1, 0)
     scatter_more(7)
     weights(0, (5, 3))
     scatter_more(6)
@@ -289,41 +329,106 @@
     for piece in range(4):
         weight_send(0, piece)
     weight(0, b, 4)
+    third_wait(0, 0)
+    fourth_send(0)
+    third_send(1, 1)
     for o in (7, 1, 6, 2):
         finish(o)
+    third_wait(0, 1)
+    partial(3, 0)
+    partial(5, 0)
+    scatter(3, 0)
+    scatter(5, 0)
     early = len(sent)
-    c_next(3, 1)
+    third_wait(1, 0)
+    fourth_send(1)
     for o in (0, 7, 1, 6, 2):
         deliver(o)
-    partial(3)
-    partial(5)
-    scatter(3)
-    scatter(5)
+    fourth_wait(0)
+    partial(4, 0)
+    scatter_more(3, 0)
+    scatter_more(5, 0)
+    scatter(4, 0)
+    drain(early)
+    third_wait(1, 1)
+    partial(3, 1)
+    partial(5, 1)
     weights(1, (5, 3))
-    drain(early)
+    scatter(3, 1)
+    scatter(5, 1)
     weight_end(0)
-    c_next(4, 1)
-    partial(4)
+    fourth_wait(1)
+    partial(4, 1)
     weight(1, 1 - b, 4)
     weight_send(1, 0)
     weight_send(1, 1)
-    scatter(4)
+    scatter(4, 1)
     weight(1, b, 4)
-    scatter_more(5)
-    scatter_more(3)
+    finish(3, 0)
+    deliver(3, 0)
+    finish(5, 0)
+    deliver(5, 0)
+    scatter_more(4, 0)
+    scatter_more(5, 1)
+    scatter_more(3, 1)
+    scatter_more(4, 1)
     weight_send(1, 2)
-    scatter_more(4)
     weight_send(1, 3)
-    for o in (5, 3, 4):
-        finish(o)
-        deliver(o)
+    for o, t in ((4, 0), (5, 1), (3, 1), (4, 1)):
+        finish(o, t)
+        deliver(o, t)
     weight_end(1)
-    for t in range(8):
-        arrived(mg_ref.at[t], o_rs.at[t])
+    far = z - k
+    batched = jnp.logical_or(jnp.abs(far) == 4, jnp.logical_or(jnp.abs(far) == 3, jnp.abs(far) == 5))
+    for j in range(8):
+
+        @pl.when(batched)
+        def _():
+            for t in range(2):
+                arrived(mg_ref.at[j, t], o_rs.at[j, t])
+
+        @pl.when(jnp.logical_not(batched))
+        def _():
+            arrived(mg_ref.at[j], o_rs.at[j, 0])
+
+    for copy in results:
+        copy.wait()
     drain(len(sent))
-    pl.when(jnp.logical_not(at_home))(finals[0].wait_send)
-    for o in range(1, 8):
-        finals[o].wait_send()
+    pl.when(jnp.logical_not(at_home))(finals[0, 0].wait_send)
+    for key, copy in finals.items():
+        if key[0]:
+            copy.wait_send()
+
+
+def place_kernel(mg_ref, wg_ref, mg_out, wg_out, mg_held, wg_held, sem):
+    parts = [(mg_ref, mg_held, mg_out, pl.ds(0, 512))]
+    parts += [(wg_ref, wg_held, wg_out, (i // 4, pl.ds(i % 4 * 64, 64))) for i in range(8)]
+    loads = [pltpu.make_async_copy(a.at[p], c.at[p], sem.at[0, i]) for i, (a, c, _, p) in enumerate(parts)]
+    stores = [pltpu.make_async_copy(c.at[p], d.at[p], sem.at[1, i]) for i, (_, c, d, p) in enumerate(parts)]
+    for load in loads:
+        load.start()
+    for load, store in zip(loads, stores):
+        load.wait()
+        store.start()
+    for store in stores:
+        store.wait()
+
+
+def place(memory_grad, weight_grad):
+    return pl.pallas_call(
+        place_kernel,
+        out_shape=(
+            jax.ShapeDtypeStruct((512, 256), jnp.bfloat16),
+            jax.ShapeDtypeStruct((2, 256, 512), F32),
+        ),
+        in_specs=[pl.BlockSpec(memory_space=pltpu.HBM)] * 2,
+        out_specs=(pl.BlockSpec(memory_space=pltpu.HBM),) * 2,
+        scratch_shapes=[
+            pltpu.VMEM((512, 256), jnp.bfloat16),
+            pltpu.VMEM((2, 256, 512), F32),
+            pltpu.SemaphoreType.DMA((2, 9)),
+        ],
+    )(memory_grad, weight_grad)
 
 
 def on_device(memory, joined_weight, joined_cotangent):
@@ -332,47 +437,49 @@
     memory_grad, weight_grad = pl.pallas_call(
         kernel,
         out_shape=(
-            jax.ShapeDtypeStruct((8, 64, 256), bf16),
+            jax.ShapeDtypeStruct((8, 2, 32, 256), bf16),
             jax.ShapeDtypeStruct((2, 256, 512), F32),
         ),
         in_specs=[pl.BlockSpec(memory_space=pltpu.HBM)] * 3,
-        out_specs=(pl.BlockSpec(memory_space=pltpu.VMEM),) * 2,
+        out_specs=(pl.BlockSpec(memory_space=pltpu.HBM),) * 2,
         scratch_shapes=[
-            pltpu.VMEM((8, 2, 512, 512), bf16),
+            pltpu.VMEM((2, 256, 512), F32),
+            dma((2, 4)),
+            pltpu.VMEM((8, 2, 4, 2, 2, 32, 512), bf16),
             pltpu.VMEM((2, 2, 256, 512), bf16),
             pltpu.VMEM((8, 64, 256), bf16),
             pltpu.VMEM((2, 8, 8, 64, 256), bf16),
-            pltpu.VMEM((8, 4, 2, 64, 256), F32),
-            pltpu.VMEM((8, 4, 2, 64, 256), F32),
-            pltpu.VMEM((8, 4, 2, 64, 256), F32),
-            pltpu.VMEM((8, 3, 2, 64, 256), F32),
-            pltpu.VMEM((8, 2, 64, 256), F32),
-            pltpu.VMEM((8, 64, 256), F32),
-            pltpu.VMEM((3, 4, 64, 256), F32),
-            pltpu.VMEM((3, 4, 64, 256), F32),
-            pltpu.VMEM((3, 3, 64, 256), F32),
-            pltpu.VMEM((8, 64, 256), bf16),
+            pltpu.VMEM((8, 4, 2, 2, 32, 256), F32),
+            pltpu.VMEM((8, 4, 2, 2, 32, 256), F32),
+            pltpu.VMEM((8, 4, 2, 2, 32, 256), F32),
+            pltpu.VMEM((8, 3, 2, 2, 32, 256), F32),
+            pltpu.VMEM((8, 2, 2, 32, 256), F32),
+            pltpu.VMEM((8, 2, 32, 256), F32),
+            pltpu.VMEM((3, 4, 2, 32, 256), F32),
+            pltpu.VMEM((3, 4, 2, 32, 256), F32),
+            pltpu.VMEM((3, 3, 2, 32, 256), F32),
+            pltpu.VMEM((8, 2, 32, 256), bf16),
             pltpu.VMEM((2, 2, 256, 512), F32),
             pltpu.VMEM((2, 256, 512), F32),
             dma((2,)),
-            dma((2, 4, 2, 2)), dma((2, 4, 2, 2)),
+            dma((2, 4, 2, 4)), dma((2, 4, 2, 4)),
             dma, dma,
             dma((8,)), dma((8,)),
             dma((8,)), dma((8,)),
             dma((8,)), dma((2, 8)), dma((8,)),
-            dma((8,)), dma((8,)),
-            dma((8, 3)), dma((8, 3)),
-            dma((8,)), dma((8,)),
-            dma((3,)), dma((3,)),
-            dma((3, 3)), dma((3, 3)),
-            dma((8,)), dma((8,)),
+            dma((8, 2)), dma((8, 2)),
+            dma((8, 3, 2)), dma((8, 3, 2)),
+            dma((8, 2)), dma((8, 2)),
+            dma((3, 2)), dma((3, 2)),
+            dma((3, 3, 2)), dma((3, 3, 2)),
+            dma((8, 2)), dma((8, 2)),
             dma((2, 4)), dma((2, 4)),
         ],
         compiler_params=pltpu.CompilerParams(
             collective_id=0, has_side_effects=True, vmem_limit_bytes=56 * 1024 * 1024
         ),
-    )(memory, joined_weight, joined_cotangent)
-    return memory_grad.reshape(512, 256), weight_grad
+    )(memory, joined_weight, joined_cotangent.reshape(2, 4, 2, 2, 32, 512))
+    return place(memory_grad.reshape(512, 256), weight_grad)
 
 
 def solution(mesh):

time: 130 us -> 127 us (0.977)
  local copies, waits for them, and re-layouts: 3.93 us -> 0 us
    unnamed x2 -> x0, local copies, waits for them, and re-layouts: 3.93 us -> none
    pallas_call x1 -> x2, Pallas kernels: 125 us -> 126 us  [the longest x1 124 us: on_device(): pl.pallas_call(kernel, out_shape=(jax.ShapeDtypeStruct((8, 2, 32, 256), b...]
where the time goes in v4:
time: 127 us
  Pallas kernels  126 us (99%)
    pallas_call x1, Pallas kernels, on_device(): pl.pallas_call(kernel, out_shape=(jax.ShapeDtypeStruct((8, 2, 32, 256), b...  124 us

profile of v4, /device:TPU:4, one launch (start us, length us, event | category | flops | bytes accessed | tf_op | source)
XLA Modules:
  0.0 126.7 jit_solution(14737419488735745820)
XLA Ops:
  0.6 123.9 %shard_map.50 = (bf16[8,2,32,256]{3,2,1,0:T(8,128)(2,1)}, f32[2,256,512]{2,1,0:T(8,128)}) custom-call(bf16[512,256]{1,0:T(8,128)(2,1)} %m_ref.1, bf16[2,256,512]{2,1,0:T(8,128)(2,1)} %w_ref.1, bf16[2,4,2,2,32,512]{5,4,3,2,1,0:T(8,128)(2,1)} %bitcast.2), custom_call_target="tpu_custom_call" | custom-call | tf_op jit(solution)/shard_map/pallas_call | solution.py:437
  124.5 2.1 %shard_map.51 = (bf16[512,256]{1,0:T(8,128)(2,1)}, f32[2,256,512]{2,1,0:T(8,128)}) custom-call(bf16[512,256]{1,0:T(8,128)(2,1)} %bitcast.3, f32[2,256,512]{2,1,0:T(8,128)} %get-tuple-element.5.wg_ref), custom_call_target="tpu_custom_call" | custom-call | tf_op jit(solution)/shard_map/pallas_call | solution.py:418

commit v5 on v4

--- a/solution.py
+++ b/solution.py
@@ -40,9 +40,6 @@
 
     c_in = pltpu.make_async_copy(c_ref, c_all.at[0], in_s.at[0])
     w_in = pltpu.make_async_copy(w_ref, w_all.at[b], in_s.at[1])
-    c_in.start()
-    w_in.start()
-
     barrier = pltpu.get_barrier_semaphore()
     greeted = plane[1:] + line[1:] + [y_pair, core_pair]
     for peer in greeted:
@@ -116,6 +113,8 @@
     m_in = pltpu.make_async_copy(m_rows(k), m_a.at[k], ma_rs.at[k])
     m_in.start()
     send(w_ref, w_all.at[b], w_ss, w_rs, y_pair)
+    c_in.start()
+    w_in.start()
 
     for o in (4, 3, 5, 2, 6, 1, 7, 0):
         piece = m_a.at[zs[o]]
@@ -346,9 +345,9 @@
         deliver(o)
     fourth_wait(0)
     partial(4, 0)
-    scatter_more(3, 0)
     scatter_more(5, 0)
     scatter(4, 0)
+    scatter_more(3, 0)
     drain(early)
     third_wait(1, 1)
     partial(3, 1)

time: 127 us -> 127 us (level)
  no operation moved by 1% of the time
where the time goes in v5:
time: 127 us
  Pallas kernels  126 us (99%)
    pallas_call x1, Pallas kernels, on_device(): pl.pallas_call(kernel, out_shape=(jax.ShapeDtypeStruct((8, 2, 32, 256), b...  124 us

profile of v5, /device:TPU:4, one launch (start us, length us, event | category | flops | bytes accessed | tf_op | source)
XLA Modules:
  0.0 126.7 jit_solution(7653977082762660386)
XLA Ops:
  0.6 123.9 %shard_map.50 = (bf16[8,2,32,256]{3,2,1,0:T(8,128)(2,1)}, f32[2,256,512]{2,1,0:T(8,128)}) custom-call(bf16[512,256]{1,0:T(8,128)(2,1)} %m_ref.1, bf16[2,256,512]{2,1,0:T(8,128)(2,1)} %w_ref.1, bf16[2,4,2,2,32,512]{5,4,3,2,1,0:T(8,128)(2,1)} %bitcast.2), custom_call_target="tpu_custom_call" | custom-call | tf_op jit(solution)/shard_map/pallas_call | solution.py:436
  124.5 2.1 %shard_map.51 = (bf16[512,256]{1,0:T(8,128)(2,1)}, f32[2,256,512]{2,1,0:T(8,128)}) custom-call(bf16[512,256]{1,0:T(8,128)(2,1)} %bitcast.3, f32[2,256,512]{2,1,0:T(8,128)} %get-tuple-element.5.wg_ref), custom_call_target="tpu_custom_call" | custom-call | tf_op jit(solution)/shard_map/pallas_call | solution.py:417

commit v6 on v4

--- a/solution.py
+++ b/solution.py
@@ -346,9 +346,9 @@
         deliver(o)
     fourth_wait(0)
     partial(4, 0)
-    scatter_more(3, 0)
     scatter_more(5, 0)
     scatter(4, 0)
+    scatter_more(3, 0)
     drain(early)
     third_wait(1, 1)
     partial(3, 1)

time: 127 us -> 127 us (level)
  no operation moved by 1% of the time
where the time goes in v6:
time: 127 us
  Pallas kernels  126 us (99%)
    pallas_call x1, Pallas kernels, on_device(): pl.pallas_call(kernel, out_shape=(jax.ShapeDtypeStruct((8, 2, 32, 256), b...  124 us

profile of v6, /device:TPU:4, one launch (start us, length us, event | category | flops | bytes accessed | tf_op | source)
XLA Modules:
  0.0 126.6 jit_solution(16082320076072678878)
XLA Ops:
  0.6 123.9 %shard_map.50 = (bf16[8,2,32,256]{3,2,1,0:T(8,128)(2,1)}, f32[2,256,512]{2,1,0:T(8,128)}) custom-call(bf16[512,256]{1,0:T(8,128)(2,1)} %m_ref.1, bf16[2,256,512]{2,1,0:T(8,128)(2,1)} %w_ref.1, bf16[2,4,2,2,32,512]{5,4,3,2,1,0:T(8,128)(2,1)} %bitcast.2), custom_call_target="tpu_custom_call" | custom-call | tf_op jit(solution)/shard_map/pallas_call | solution.py:437
  124.5 2.1 %shard_map.51 = (bf16[512,256]{1,0:T(8,128)(2,1)}, f32[2,256,512]{2,1,0:T(8,128)}) custom-call(bf16[512,256]{1,0:T(8,128)(2,1)} %bitcast.3, f32[2,256,512]{2,1,0:T(8,128)} %get-tuple-element.5.wg_ref), custom_call_target="tpu_custom_call" | custom-call | tf_op jit(solution)/shard_map/pallas_call | solution.py:418
